TPU v7x, 32 devices: a whole 2x2x4 slice. The times are simulated.
32 devices in a mesh: rep: 2 (over x), ep: 16 (over z, y, core).
Axes of the slice: x: 2, y: 2, z: 4, core: 2. Of those that a mesh axis runs over, the one named last changes fastest.
Arguments:
- tokens: bfloat16 [4096, 1024], P(('rep', 'ep')), may hold values from -6 to 6
- query: bfloat16 [4096, 1024], P(('rep', 'ep')), may hold values from -6 to 6
- expert_ids: int32 [4096, 6], P(('rep', 'ep')), may hold values from 0 to 15, all different within a row; in each aligned block of 128 rows (0 to 127, 128 to 255, ...) at most 49 rows name the same one
- gate_probs: bfloat16 [4096, 6], P(('rep', 'ep')), may hold values from 0.049804688 to 0.34960938
- w_gate_up: bfloat16 [16, 1024, 1408], P('ep'), may hold values from -0.1875 to 0.1875
- w_down: bfloat16 [16, 1024, 704], P('ep', 'rep'), may hold values from -0.1875 to 0.1875
- dir_gate: bfloat16 [16, 1024, 704], P('ep', 'rep'), may hold values from -0.1875 to 0.1875
Outputs:
- hvp_gate_up: float32 [16, 1024, 1408], P('ep', 'rep')
Inputs may be any that keep to these rules, and one draw needn't show every extreme that they name: `expert_ids`: each row names 6 different experts; among the rows of one device no expert is named by more than 49 pairs, and in every draw some expert is named by exactly 49 pairs of some device.
All inputs are finite; a program needn't handle non-finite values.
Results may differ from a plain program's by a relative error of at most 0.015.
Values may be sent and summed in bfloat16 or wider, within the bound.
A program may use at most 64 MiB of HBM per device.

v0:
```python
import jax
import jax.numpy as jnp
from jax import lax
from jax.sharding import PartitionSpec as P


def make_factors(gate_pre, up_pre, error_hidden, tangent):
    sigmoid_a = 1.0 / (1.0 + jnp.exp(-gate_pre))
    slope = sigmoid_a * (1.0 + gate_pre * (1.0 - sigmoid_a))
    bend = sigmoid_a * (1.0 - sigmoid_a) * (2.0 + gate_pre * (1.0 - 2.0 * sigmoid_a))
    return jnp.concatenate(
        [error_hidden * up_pre * bend * tangent, error_hidden * slope * tangent], axis=1
    ).astype(jnp.bfloat16)


def on_device(tokens, query, expert_ids, gate_probs, w_gate_up, w_down, dir_gate):
    experts = lax.axis_size("ep")
    tok_count, top_count = expert_ids.shape
    model_width = tokens.shape[1]
    hidden_width = dir_gate.shape[2]
    capacity = tok_count * top_count // experts + 1
    pair_count = tok_count * top_count
    flat_ids = expert_ids.reshape(-1)
    onehot = (flat_ids[:, None] == jnp.arange(experts, dtype=jnp.int32)[None, :]).astype(
        jnp.bfloat16
    )
    pair_numbers = jnp.arange(pair_count, dtype=jnp.int32)
    before = (pair_numbers[:, None] > pair_numbers[None, :]).astype(jnp.bfloat16)
    earlier = jnp.dot(before, onehot, preferred_element_type=jnp.float32)
    slot_index = jnp.sum(onehot.astype(jnp.float32) * earlier, axis=1).astype(jnp.int32)
    slot_target = flat_ids * capacity + slot_index
    slot_numbers = jnp.arange(experts * capacity, dtype=jnp.int32)
    slot_match = (slot_numbers[:, None] == slot_target[None, :]).reshape(
        experts * capacity, tok_count, top_count
    )
    place_tokens = jnp.sum(slot_match.astype(jnp.float32), axis=2).astype(jnp.bfloat16)
    flat_gates = gate_probs.astype(jnp.float32)
    place_gates = jnp.sum(jnp.where(slot_match, flat_gates[None, :, :], jnp.float32(0.0)), axis=2)
    send_tokens = (
        jnp.dot(place_tokens, tokens, preferred_element_type=jnp.float32)
        .astype(jnp.bfloat16)
        .reshape(experts, capacity, model_width)
    )
    send_scaled = (
        jnp.dot(
            place_gates,
            query.astype(jnp.float32),
            precision=lax.Precision.HIGHEST,
            preferred_element_type=jnp.float32,
        )
        .astype(jnp.bfloat16)
        .reshape(experts, capacity, model_width)
    )
    got_tokens, got_scaled = (
        lax.all_to_all(send_tokens, "ep", split_axis=0, concat_axis=0, tiled=True),
        lax.all_to_all(send_scaled, "ep", split_axis=0, concat_axis=0, tiled=True),
    )
    token_rows = got_tokens.reshape(-1, model_width)
    scaled = got_scaled.reshape(-1, model_width)
    pre_act = jnp.dot(token_rows, w_gate_up[0], preferred_element_type=jnp.float32)
    error_part = jnp.dot(
        scaled,
        lax.all_gather(w_down, "rep", axis=1, tiled=True)[0],
        preferred_element_type=jnp.float32,
    )
    tangent_part = jnp.dot(
        token_rows,
        lax.all_gather(dir_gate, "rep", axis=1, tiled=True)[0],
        preferred_element_type=jnp.float32,
    )
    factors = make_factors(
        pre_act[:, :hidden_width], pre_act[:, hidden_width:], error_part, tangent_part
    )
    own_rows = lax.psum_scatter(
        lax.dot_general(
            token_rows, factors, (((0,), (0,)), ((), ())), preferred_element_type=jnp.float32
        ).astype(jnp.bfloat16),
        "rep",
        scatter_dimension=0,
        tiled=True,
    ).astype(jnp.float32)
    return own_rows[None]


def solution(mesh):
    return jax.shard_map(
        on_device,
        mesh=mesh,
        in_specs=(
            P(("rep", "ep"), None),
            P(("rep", "ep"), None),
            P(("rep", "ep"), None),
            P(("rep", "ep"), None),
            P("ep", None, None),
            P("ep", "rep", None),
            P("ep", "rep", None),
        ),
        out_specs=P("ep", "rep", None),
        check_vma=False,
    )
```

profile of v0, /device:TPU:0, one launch (start us, length us, event | category | flops | bytes accessed | tf_op | source)
XLA Modules:
  0.0 189.4 jit_solution(4521595848507766517)
XLA Ops:
  6.5 0.8 convert_element_type.45
  7.4 0.8 copy.18
  8.2 0.1 eq.30
  8.3 0.3 fusion.20
  8.7 0.1 convert_element_type.41
  8.8 0.1 copy.19
  8.9 0.7 multiply_add_fusion
  9.6 0.5 select_reduce_fusion
  10.1 3.5 %convolution_convert_fusion.1 = bf16[784,1024]{1,0:T(8,128)(2,1)} fusion(f32[784,128]{1,0:T(8,128)S(1)} %get-tuple-element.5, bf16[128,1024]{1,0:T(8,128)(2,1)} %param.8), kind=kOutput, calls=%fused_computation.24 | convolution fusion | flops 1233928192 | bytes 2269184 | tf_op jit(solution)/shard_map/dot_general | solution.py:45
  13.7 2.6 %reshape.36 = bf16[16,49,1024]{2,1,0:T(8,128)(2,1)} reshape(bf16[784,1024]{1,0:T(8,128)(2,1)} %convolution_convert_fusion.1) | data formatting | bytes 3211264 | tf_op jit(solution)/shard_map/reshape | solution.py:52
  16.3 7.6 %all-to-all-start.1 = ((bf16[16,49,1024]{2,1,0:T(8,128)(2,1)}), bf16[16,49,1024]{2,1,0:T(8,128)(2,1)}, u32[]{:S(2)}, u32[]{:S(2)}) async-start(bf16[16,49,1024]{2,1,0:T(8,128)(2,1)} %reshape.36), calls=%async_computation.1 | async-start | bytes 3670016 | tf_op jit(solution)/shard_map/all_to_all | solution.py:56
  23.9 1.7 convolution_convert_fusion.2
  25.6 2.6 %reshape.34 = bf16[16,49,1024]{2,1,0:T(8,128)(2,1)} reshape(bf16[784,1024]{1,0:T(8,128)(2,1)} %convolution_convert_fusion.2) | data formatting | bytes 3211264 | tf_op jit(solution)/shard_map/reshape | solution.py:42
  28.2 32.3 %all-to-all-done.1 = bf16[16,49,1024]{2,1,0:T(8,128)(2,1)} async-done(((bf16[16,49,1024]{2,1,0:T(8,128)(2,1)}), bf16[16,49,1024]{2,1,0:T(8,128)(2,1)}, u32[]{:S(2)}, u32[]{:S(2)}) %all-to-all-start.1) | async-done | bytes 1605664 | tf_op jit(solution)/shard_map/all_to_all | solution.py:56
  60.4 10.2 %all-to-all-start = ((bf16[16,49,1024]{2,1,0:T(8,128)(2,1)}), bf16[16,49,1024]{2,1,0:T(8,128)(2,1)}, u32[]{:S(2)}, u32[]{:S(2)}) async-start(bf16[16,49,1024]{2,1,0:T(8,128)(2,1)} %reshape.34), calls=%async_computation | async-start | bytes 3670016 | tf_op jit(solution)/shard_map/all_to_all | solution.py:55
  70.7 0.0 all-gather.3.cloned.1.call-start
  70.7 0.7 all-gather.3.cloned.1.call-update
  71.4 0.0 all-gather.5.cloned.1.call-start
  71.4 0.7 all-gather.5.cloned.1.call-update
  72.1 0.0 reduce-scatter.2.cloned.1.call-start
  72.2 2.6 %reshape.37 = bf16[784,1024]{1,0:T(8,128)(2,1)} reshape(bf16[16,49,1024]{2,1,0:T(8,128)(2,1)} %all-to-all-done.1) | data formatting | bytes 3211264 | tf_op jit(solution)/shard_map/reshape | solution.py:59
  74.8 32.5 %all-to-all-done = bf16[16,49,1024]{2,1,0:T(8,128)(2,1)} async-done(((bf16[16,49,1024]{2,1,0:T(8,128)(2,1)}), bf16[16,49,1024]{2,1,0:T(8,128)(2,1)}, u32[]{:S(2)}, u32[]{:S(2)}) %all-to-all-start) | async-done | bytes 1605664 | tf_op jit(solution)/shard_map/all_to_all | solution.py:55
  107.3 2.8 %reshape.35 = bf16[784,1024]{1,0:T(8,128)(2,1)} reshape(bf16[16,49,1024]{2,1,0:T(8,128)(2,1)} %all-to-all-done) | data formatting | bytes 3211264 | tf_op jit(solution)/shard_map/reshape | solution.py:58
  110.0 4.9 %fusion.17 = f32[784,704]{1,0:T(8,128)} fusion(bf16[784,1024]{1,0:T(8,128)(2,1)} %reshape.37, bf16[1,1024,704]{1,2,0:T(8,128)(2,1)} %all-gather.3.cloned.1.call-done), kind=kOutput, calls=%fused_computation.29 | convolution fusion | flops 1130364928 | bytes 5255168 | tf_op jit(solution)/shard_map/dot_general | solution.py:61
  114.9 0.0 copy-done.1
  114.9 4.2 %fusion = f32[784,1408]{1,0:T(8,128)} fusion(bf16[784,1024]{1,0:T(8,128)(2,1)S(1)} %copy-done.1, bf16[1,1024,1408]{2,1,0:T(8,128)(2,1)S(1)} %copy-done), kind=kOutput, calls=%fused_computation.3 | convolution fusion | flops 2260729856 | bytes 8904704 | tf_op jit(solution)/shard_map/dot_general | solution.py:60
  119.1 8.2 %all-gather.5.cloned.1.call-done = bf16[1,1024,704]{1,2,0:T(8,128)(2,1)} async-done(((bf16[1,512,704]{1,2,0:T(8,128)(2,1)}), bf16[1,1024,704]{1,2,0:T(8,128)(2,1)}) %all-gather.5.cloned.1.call-update) | async-done | bytes 1441808 | tf_op jit(solution)/shard_map/all_gather | solution.py:68
  127.4 6.6 %fusion.5 = (bf16[784,704]{1,0:T(8,128)(2,1)S(1)}, bf16[784,704]{1,0:T(8,128)(2,1)S(1)}) fusion(f32[784,704]{1,0:T(8,128)} %fusion.17, f32[784,1408]{1,0:T(8,128)} %fusion, bf16[784,1024]{1,0:T(8,128)(2,1)} %reshape.35, bf16[1,1024,704]{1,2,0:T(8,128)(2,1)} %all-gather.5.cloned.1.call-done), kind=kOutput, calls=%fused_computation.8 | convolution fusion | flops 1141403648 | bytes 11878400 | tf_op jit(solution)/shard_map/dot_general | solution.py:66
  134.0 5.1 %convolution_convert_fusion = bf16[1024,1408]{1,0:T(8,128)(2,1)} fusion(bf16[784,1024]{1,0:T(8,128)(2,1)S(1)} %copy-done.2, bf16[784,704]{1,0:T(8,128)(2,1)S(1)} %get-tuple-element.8, bf16[784,704]{1,0:T(8,128)(2,1)S(1)} %get-tuple-element.7), kind=kOutput, calls=%fused_computation | convolution fusion | flops 2266587136 | bytes 6696960 | tf_op jit(solution)/shard_map/dot_general | solution.py:75
  139.1 0.0 reduce-scatter.2.cloned.1.call-update
  139.1 40.6 %reduce-scatter.2.cloned.1.call-done = bf16[512,1408]{1,0:T(8,128)(2,1)} async-done(((bf16[1024,1408]{1,0:T(8,128)(2,1)}), bf16[512,1408]{1,0:T(8,128)(2,1)}) %reduce-scatter.2.cloned.1.call-update) | async-done | bytes 1441808 | tf_op jit(solution)/shard_map/reduce_scatter | solution.py:74
  179.8 3.1 %bitcast_convert_fusion = f32[1,512,1408]{2,1,0:T(8,128)} fusion(bf16[512,1408]{1,0:T(8,128)(2,1)} %reduce-scatter.2.cloned.1.call-done), kind=kLoop, calls=%fused_computation.26 | loop fusion | flops 720896 | bytes 4325376 | tf_op jit(solution)/shard_map/broadcast_in_dim | solution.py:82
  (9 shorter events, 0.0 us)
Async XLA Ops:
  6.5 108.4 %copy-start = (bf16[1,1024,1408]{2,1,0:T(8,128)(2,1)S(1)}, bf16[1,1024,1408]{2,1,0:T(8,128)(2,1)}, u32[]{:S(2)}) copy-start(bf16[1,1024,1408]{2,1,0:T(8,128)(2,1)} %param.11) | copy-start | bytes 8650756
  16.3 7.6 %copy-start.3 = (bf16[128,1024]{1,0:T(8,128)(2,1)S(1)}, bf16[128,1024]{1,0:T(8,128)(2,1)}, u32[]{:S(2)}) copy-start(bf16[128,1024]{1,0:T(8,128)(2,1)} %param.7) | copy-start | bytes 786436
  16.3 44.2 %all-to-all-start.1 = ((bf16[16,49,1024]{2,1,0:T(8,128)(2,1)}), bf16[16,49,1024]{2,1,0:T(8,128)(2,1)}, u32[]{:S(2)}, u32[]{:S(2)}) async-start(bf16[16,49,1024]{2,1,0:T(8,128)(2,1)} %reshape.36), calls=%async_computation.1 | async-start | bytes 3670016 | tf_op jit(solution)/shard_map/all_to_all | solution.py:56
  60.4 46.8 %all-to-all-start = ((bf16[16,49,1024]{2,1,0:T(8,128)(2,1)}), bf16[16,49,1024]{2,1,0:T(8,128)(2,1)}, u32[]{:S(2)}, u32[]{:S(2)}) async-start(bf16[16,49,1024]{2,1,0:T(8,128)(2,1)} %reshape.34), calls=%async_computation | async-start | bytes 3670016 | tf_op jit(solution)/shard_map/all_to_all | solution.py:55
  70.7 39.4 %all-gather.3.cloned.1.call-start = ((), (), s32[]{:S(2)}) async-start(), calls=%async_computation.3 | async-start | bytes 2162688 | tf_op jit(solution)/shard_map/all_gather | solution.py:63
  71.4 56.0 %all-gather.5.cloned.1.call-start = ((), (), s32[]{:S(2)}) async-start(), calls=%async_computation.4 | async-start | bytes 2162688 | tf_op jit(solution)/shard_map/all_gather | solution.py:68
  72.1 107.6 %reduce-scatter.2.cloned.1.call-start = ((), (), s32[]{:S(2)}) async-start(), calls=%async_computation.5 | async-start | bytes 4325376 | tf_op jit(solution)/shard_map/reduce_scatter | solution.py:74
  110.0 4.9 %copy-start.1 = (bf16[784,1024]{1,0:T(8,128)(2,1)S(1)}, bf16[784,1024]{1,0:T(8,128)(2,1)}, u32[]{:S(2)}) copy-start(bf16[784,1024]{1,0:T(8,128)(2,1)} %reshape.35) | copy-start | bytes 4816900
  127.4 6.7 %copy-start.2 = (bf16[784,1024]{1,0:T(8,128)(2,1)S(1)}, bf16[784,1024]{1,0:T(8,128)(2,1)}, u32[]{:S(2)}) copy-start(bf16[784,1024]{1,0:T(8,128)(2,1)} %reshape.35) | copy-start | bytes 4816900
Sparse Core Ops, SparseCore 0:
  73.0 26.9 all-gather.2
  101.6 25.7 all-gather.4
  139.3 40.4 reduce-scatter.1
where the time goes:
time: 190 us; the launch traced here: 189 us
  waiting for transfers between devices  115 us (61%)
  matrix products  26.4 us (14%)
  starting transfers between devices  17.9 us (9%)
  between operations  13.2 us (7%)
  local copies, waits for them, and re-layouts  11.8 us (6%)
  other arithmetic  5.2 us (3%)
    reduce_scatter x1, waiting for transfers between devices, on_device(): lax.psum_scatter(lax.dot_general(token_rows, factors, (((0,), (0,)), ((),...  40.6 us
    all_to_all x1, waiting for transfers between devices, on_device(): lax.all_to_all(send_tokens, 'ep', split_axis=0, concat_axis=0, tiled=True)  32.5 us
    all_to_all x1, waiting for transfers between devices, on_device(): lax.all_to_all(send_scaled, 'ep', split_axis=0, concat_axis=0, tiled=True)  32.3 us
    all_to_all x1, starting transfers between devices, on_device(): lax.all_to_all(send_tokens, 'ep', split_axis=0, concat_axis=0, tiled=True)  10.2 us
    all_gather x1, waiting for transfers between devices, on_device(): lax.all_gather(dir_gate, 'rep', axis=1, tiled=True)[0]  8.24 us
    all_to_all x1, starting transfers between devices, on_device(): lax.all_to_all(send_scaled, 'ep', split_axis=0, concat_axis=0, tiled=True)  7.56 us
    dot_general x1, matrix products, on_device(): jnp.dot(token_rows, lax.all_gather(dir_gate, 'rep', axis=1, tiled=True)[0...  6.64 us
    dot_general x1, matrix products, on_device(): lax.dot_general(token_rows, factors, (((0,), (0,)), ((), ())), preferred_...  5.06 us
  transfers between devices with their start and end apart: 5, of which 4 were waited for; matrix products, arithmetic and copies ran while one was open for 10% of the time, Pallas kernels for 0%

commit v1 on v0

v1 whole, which is shorter than its diff:
```python
import jax
import jax.numpy as jnp
from jax import lax
from jax.sharding import PartitionSpec as P


def make_factors(gate_pre, up_pre, error_hidden, tangent):
    sigmoid_a = 1.0 / (1.0 + jnp.exp(-gate_pre))
    slope = sigmoid_a * (1.0 + gate_pre * (1.0 - sigmoid_a))
    bend = sigmoid_a * (1.0 - sigmoid_a) * (2.0 + gate_pre * (1.0 - 2.0 * sigmoid_a))
    common = error_hidden * tangent
    return (common * up_pre * bend).astype(jnp.bfloat16), (common * slope).astype(jnp.bfloat16)


def dot(a, b, contract=((1,), (0,))):
    return lax.dot_general(a, b, (contract, ((), ())), preferred_element_type=jnp.float32)


def on_device(tokens, query, expert_ids, gate_probs, w_gate_up, w_down, dir_gate):
    experts = lax.axis_size("ep")
    reps = lax.axis_size("rep")
    me = lax.axis_index("ep")
    tok_count, top_count = expert_ids.shape
    model_width = tokens.shape[1]
    hidden_width = dir_gate.shape[2]
    capacity = tok_count * top_count // experts + 1
    capacity = -(-capacity // 16) * 16

    if reps == 2:
        pairs = [(0, 1), (1, 0)]
        w_down_far = lax.ppermute(w_down[0], "rep", pairs)
        dir_far = lax.ppermute(dir_gate[0], "rep", pairs)

    meta = jnp.concatenate([expert_ids.astype(jnp.bfloat16), gate_probs], axis=1).T
    meta = lax.all_gather(meta, "ep", axis=0, tiled=False)
    all_tokens = lax.all_gather(tokens, "ep", axis=0, tiled=False)
    all_query = lax.all_gather(query, "ep", axis=0, tiled=False)

    routed = (meta[:, :top_count].astype(jnp.int32) == me).astype(jnp.float32)
    gates = jnp.sum(routed * meta[:, top_count:].astype(jnp.float32), axis=1)
    chosen = jnp.sum(routed, axis=1)
    order = jnp.arange(tok_count, dtype=jnp.int32)
    before = (order[:, None] < order[None, :]).astype(jnp.bfloat16)
    rank = dot(chosen.astype(jnp.bfloat16), before)
    slots = jnp.arange(capacity, dtype=jnp.float32)
    match = (rank[:, None, :] == slots[None, :, None]) & (chosen[:, None, :] > 0.5)
    place = match.astype(jnp.bfloat16)
    gate_rows = jnp.sum(jnp.where(match, gates[:, None, :], 0.0), axis=2)

    def pick(rows):
        return lax.dot_general(
            place, rows, (((2,), (1,)), ((0,), (0,))), preferred_element_type=jnp.float32
        )

    token_rows = pick(all_tokens).astype(jnp.bfloat16).reshape(-1, model_width)
    scaled = (gate_rows[:, :, None] * pick(all_query)).astype(jnp.bfloat16).reshape(-1, model_width)

    pre_act = dot(token_rows, w_gate_up[0])
    if reps == 2:
        half = model_width // 2
        own_at = lax.axis_index("rep") * half
        far_at = half - own_at

        def columns(array, at):
            return lax.dynamic_slice_in_dim(array, at, half, axis=1)

        near_tokens, far_tokens = columns(token_rows, own_at), columns(token_rows, far_at)
        error = dot(columns(scaled, own_at), w_down[0]) + dot(columns(scaled, far_at), w_down_far)
        tangent = dot(near_tokens, dir_gate[0]) + dot(far_tokens, dir_far)
        parts = make_factors(
            pre_act[:, :hidden_width], pre_act[:, hidden_width:], error, tangent
        )
        first = ((0,), (0,))
        got = [
            lax.ppermute(dot(far_tokens, part, first).astype(jnp.bfloat16), "rep", pairs)
            for part in parts
        ]
        kept = [dot(near_tokens, part, first) for part in parts]
        return jnp.concatenate(
            [k + g.astype(jnp.float32) for k, g in zip(kept, got)], axis=1
        )[None]
    error = dot(scaled, lax.all_gather(w_down[0], "rep", axis=0, tiled=True))
    tangent = dot(token_rows, lax.all_gather(dir_gate[0], "rep", axis=0, tiled=True))
    factors = jnp.concatenate(
        make_factors(pre_act[:, :hidden_width], pre_act[:, hidden_width:], error, tangent), axis=1
    )
    own_rows = lax.psum_scatter(
        dot(token_rows, factors, ((0,), (0,))).astype(jnp.bfloat16),
        "rep",
        scatter_dimension=0,
        tiled=True,
    ).astype(jnp.float32)
    return own_rows[None]


def solution(mesh):
    return jax.shard_map(
        on_device,
        mesh=mesh,
        in_specs=(
            P(("rep", "ep"), None),
            P(("rep", "ep"), None),
            P(("rep", "ep"), None),
            P(("rep", "ep"), None),
            P("ep", None, None),
            P("ep", "rep", None),
            P("ep", "rep", None),
        ),
        out_specs=P("ep", "rep", None),
        check_vma=False,
    )
```

time: 190 us -> 176 us (0.926)
  blocking collectives: 0 us -> 22.5 us
  starting transfers between devices: 17.9 us -> 5.27 us
  waiting for transfers between devices: 115 us -> 103 us
  local copies, waits for them, and re-layouts: 11.8 us -> 5.3 us
  matrix products: 26.4 us -> 22.8 us
    all_to_all x2 -> x0, waiting for transfers between devices: 64.7 us -> none  [the longest x1 32.5 us: on_device(): lax.all_to_all(send_tokens, 'ep', split_axis=0, concat_axis=0, tiled=True)]
    all_gather x2, waiting for transfers between devices: 8.25 us -> 72 us  [the longest x1 44.4 us: on_device(): all_tokens = lax.all_gather(tokens, 'ep', axis=0, tiled=False)]
    reduce_scatter x1 -> x0, waiting for transfers between devices: 40.6 us -> none  [on_device(): lax.psum_scatter(lax.dot_general(token_rows, factors, (((0,), (0,)), ((),...]
    ppermute x0 -> x4, waiting for transfers between devices: none -> 29.8 us  [the longest x2 29.8 us: on_device(): lax.ppermute(dot(far_tokens, part, first).astype(jnp.bfloat16), 'rep', pa...]
    all_gather x0 -> x1, blocking collectives: none -> 22.5 us  [on_device(): meta = lax.all_gather(meta, 'ep', axis=0, tiled=False)]
    all_to_all x2 -> x0, starting transfers between devices: 17.8 us -> none  [the longest x1 10.2 us: on_device(): lax.all_to_all(send_tokens, 'ep', split_axis=0, concat_axis=0, tiled=True)]
    reshape x4 -> x0, local copies, waits for them, and re-layouts: 10.6 us -> none  [the longest x1 2.78 us: on_device(): token_rows = got_tokens.reshape(-1, model_width)]
    ppermute x0 -> x4, starting transfers between devices: none -> 5.23 us  [the longest x1 3 us: on_device(): dir_far = lax.ppermute(dir_gate[0], 'rep', pairs)]
  transfers between devices with their start and end apart: 5 -> 6, of which waited for: 4 -> 4; matrix products, arithmetic and copies ran while one was open for 10% -> 11% of each run, Pallas kernels for 0% -> 0%
where the time goes in v1:
time: 176 us
  waiting for transfers between devices  103 us (59%)
  matrix products  22.8 us (13%)
  blocking collectives  22.5 us (13%)
  between operations  13.6 us (8%)
  local copies, waits for them, and re-layouts  5.3 us (3%)
  starting transfers between devices  5.27 us (3%)
  other arithmetic  3.53 us (2%)
    all_gather x1, waiting for transfers between devices, on_device(): all_tokens = lax.all_gather(tokens, 'ep', axis=0, tiled=False)  44.4 us
    ppermute x2, waiting for transfers between devices, on_device(): lax.ppermute(dot(far_tokens, part, first).astype(jnp.bfloat16), 'rep', pa...  29.8 us
    all_gather x1, waiting for transfers between devices, on_device(): all_query = lax.all_gather(query, 'ep', axis=0, tiled=False)  27.6 us
    all_gather x1, blocking collectives, on_device(): meta = lax.all_gather(meta, 'ep', axis=0, tiled=False)  22.5 us
    dot_general x10, matrix products, dot(): lax.dot_general(a, b, (contract, ((), ())), preferred_element_type=jnp.fl...  16.8 us
    dot_general x2, matrix products, pick(): lax.dot_general(place, rows, (((2,), (1,)), ((0,), (0,))), preferred_elem...  5.94 us
  transfers between devices with their start and end apart: 6, of which 4 were waited for; matrix products, arithmetic and copies ran while one was open for 11% of the time, Pallas kernels for 0%

profile of v1, /device:TPU:0, one launch (start us, length us, event | category | flops | bytes accessed | tf_op | source)
XLA Modules:
  0.0 176.1 jit_solution(18110929206020527439)
XLA Ops:
  6.5 0.7 all-gather.9.cloned.1.call-update
  7.3 0.0 all-gather.7.cloned.1.call-start
  7.3 0.7 all-gather.7.cloned.1.call-update
  8.0 3.0 %collective-permute-start.1 = (bf16[512,704]{0,1:T(8,128)(2,1)}, bf16[512,704]{0,1:T(8,128)(2,1)}, u32[]{:S(2)}, u32[]{:S(2)}) collective-permute-start(bf16[512,704]{0,1:T(8,128)(2,1)} %bitcast.40), channel_id=1, source_target_pairs={{0,16},{16,0},{1,17},{17,1},{2,18},{18,2},{3,19},{19,3},{4,20},{20... | collective-permute-start | bytes 2162696 | tf_op jit(solution)/shard_map/ppermute | solution.py:32
  11.0 0.1 collective-permute-start
  11.1 0.7 convert_element_type.41
  11.8 0.7 maximum_bitcast_fusion.1
  12.5 22.5 %all-gather.3 = bf16[16,12,128]{2,1,0:T(8,128)(2,1)S(1)} all-gather(bf16[1,12,128]{2,1,0:T(8,128)(2,1)S(1)} %maximum_bitcast_fusion.1), channel_id=2, replica_groups=mesh['rep'=2,'ep'=16] {'ep'}, dimensions={0}, use_global_device_ids=true | all-gather | bytes 52224 | tf_op jit(solution)/shard_map/all_gather | solution.py:35
  34.9 0.1 select_reduce_fusion.1
  35.0 0.1 fusion.33
  35.1 0.2 select_reduce_fusion
  35.4 27.6 %all-gather.9.cloned.1.call-done = bf16[2048,1024]{1,0:T(8,128)(2,1)} async-done(((bf16[128,1024]{1,0:T(8,128)(2,1)}), bf16[2048,1024]{1,0:T(8,128)(2,1)}) %all-gather.9.cloned.1.call-update) | async-done | bytes 4194320 | tf_op jit(solution)/shard_map/all_gather | solution.py:37
  63.0 3.0 %multiply_convert_fusion = bf16[16,64,1024]{2,1,0:T(8,128)(2,1)S(1)} fusion(bf16[16,128,1024]{2,1,0:T(8,128)(2,1)} %bitcast.28, f32[16,64]{1,0:T(8,128)S(1)} %select_reduce_fusion, f32[16,128]{1,0:T(8,128)S(1)} %fusion.33, pred[16,128]{1,0:T(8,128)(4,1)S(1)} %broadcast_compare_fusion), kind=kOutput, calls=%fused_computation | convolution fusion | flops 270794752 | bytes 6305792 | tf_op jit(solution)/shard_map/dot_general | solution.py:51
  66.0 1.3 copy-done.1
  67.3 2.5 %fusion.11 = f32[1024,704]{0,1:T(8,128)} fusion(bf16[1024,1024]{1,0:T(8,128)(2,1)S(1)} %bitcast.37, s32[]{:T(128)S(6)} %select_n.12, bf16[1,512,704]{1,2,0:T(8,128)(2,1)S(1)} %copy-done.3), kind=kOutput, calls=%fused_computation.23 | convolution fusion | flops 738197504 | bytes 4653060 | tf_op jit(solution)/shard_map/dot_general | solution.py:16
  69.8 44.4 %all-gather.7.cloned.1.call-done = bf16[2048,1024]{1,0:T(8,128)(2,1)} async-done(((bf16[128,1024]{1,0:T(8,128)(2,1)}), bf16[2048,1024]{1,0:T(8,128)(2,1)}) %all-gather.7.cloned.1.call-update) | async-done | bytes 4194320 | tf_op jit(solution)/shard_map/all_gather | solution.py:36
  114.2 3.0 %convolution_convert_fusion = bf16[16,64,1024]{2,1,0:T(8,128)(2,1)S(1)} fusion(bf16[16,128,1024]{2,1,0:T(8,128)(2,1)} %bitcast.29, f32[16,128]{1,0:T(8,128)S(1)} %fusion.33, pred[16,128]{1,0:T(8,128)(4,1)S(1)} %broadcast_compare_fusion), kind=kOutput, calls=%fused_computation.16 | convolution fusion | flops 269746176 | bytes 6301696 | tf_op jit(solution)/shard_map/dot_general | solution.py:51
  117.2 1.0 fusion.20
  118.2 0.6 copy-done.2
  118.8 2.1 %fusion.9 = f32[1024,704]{0,1:T(8,128)S(1)} fusion(bf16[512,704]{0,1:T(8,128)(2,1)} %collective-permute-done, bf16[1024,1024]{1,0:T(8,128)(2,1)S(1)} %bitcast.38, s32[]{:T(128)S(6)} %select_n.14), kind=kOutput, calls=%fused_computation.21 | convolution fusion | flops 738197504 | bytes 4653060 | tf_op jit(solution)/shard_map/dot_general | solution.py:16
  120.9 3.3 %fusion.7 = f32[1024,1408]{0,1:T(8,128)S(1)} fusion(bf16[1024,1024]{1,0:T(8,128)(2,1)S(1)} %bitcast.31, bf16[1,1024,1408]{2,1,0:T(8,128)(2,1)S(1)} %copy-done), kind=kOutput, calls=%fused_computation.12 | convolution fusion | flops 2952790016 | bytes 10747904 | tf_op jit(solution)/shard_map/dot_general | solution.py:16
  124.2 4.1 %fusion.2 = (bf16[1024,704]{0,1:T(8,128)(2,1)S(1)}, bf16[1024,704]{0,1:T(8,128)(2,1)S(1)}) fusion(f32[1024,1408]{0,1:T(8,128)S(1)} %fusion.7, f32[1024,704]{0,1:T(8,128)S(1)} %fusion.20, bf16[512,704]{0,1:T(8,128)(2,1)} %collective-permute-done.1, bf16[1024,1024]{1,0:T(8,128)(2,1)S(1)} %bitcast.32, s32[]{:T(128)S(6)} %select_n.14, ...), kind=kOutput, calls=%fused_computation.5 | convolution fusion | flops 753336320 | bytes 19070980 | tf_op jit(solution)/shard_map/dot_general | solution.py:16
  128.3 0.9 convolution_convert_fusion.1
  129.3 1.5 collective-permute-start.3
  130.8 0.9 convolution_convert_fusion.2
  131.7 0.6 collective-permute-start.2
  132.3 16.0 %collective-permute-done.3 = bf16[512,704]{0,1:T(8,128)(2,1)S(1)} collective-permute-done((bf16[512,704]{0,1:T(8,128)(2,1)S(1)}, bf16[512,704]{0,1:T(8,128)(2,1)S(1)}, u32[]{:S(2)}, u32[]{:S(2)}) %collective-permute-start.3) | collective-permute-done | bytes 720928 | tf_op jit(solution)/shard_map/ppermute | solution.py:75
  148.3 0.9 convert_add_fusion
  149.2 13.8 %collective-permute-done.2 = bf16[512,704]{0,1:T(8,128)(2,1)S(1)} collective-permute-done((bf16[512,704]{0,1:T(8,128)(2,1)S(1)}, bf16[512,704]{0,1:T(8,128)(2,1)S(1)}, u32[]{:S(2)}, u32[]{:S(2)}) %collective-permute-start.2) | collective-permute-done | bytes 720928 | tf_op jit(solution)/shard_map/ppermute | solution.py:75
  163.1 0.9 convert_add_fusion.1
  164.0 1.9 %maximum_bitcast_fusion = f32[1,512,1408]{1,2,0:T(8,128)} fusion(f32[512,704]{0,1:T(8,128)S(1)} %convert_add_fusion, f32[512,704]{0,1:T(8,128)S(1)} %convert_add_fusion.1), kind=kLoop, calls=%fused_computation.11 | loop fusion | flops 720896 | bytes 5767168 | tf_op jit(solution)/shard_map/broadcast_in_dim | solution.py:79
  165.9 3.4 %copy.13 = f32[1,512,1408]{2,1,0:T(8,128)} copy(f32[1,512,1408]{1,2,0:T(8,128)} %maximum_bitcast_fusion) | data formatting | bytes 5767168 | tf_op jit(solution)/shard_map/broadcast_in_dim | solution.py:79
  (14 shorter events, 0.0 us)
Async XLA Ops:
  6.5 114.3 %copy-start = (bf16[1,1024,1408]{2,1,0:T(8,128)(2,1)S(1)}, bf16[1,1024,1408]{2,1,0:T(8,128)(2,1)}, u32[]{:S(2)}) copy-start(bf16[1,1024,1408]{2,1,0:T(8,128)(2,1)} %param.11) | copy-start | bytes 8650756
  6.5 56.4 %all-gather.9.cloned.1.call-start = ((), (), s32[]{:S(2)}) async-start(), calls=%async_computation.1 | async-start | bytes 4456448 | tf_op jit(solution)/shard_map/all_gather | solution.py:37
  7.3 107.0 %all-gather.7.cloned.1.call-start = ((), (), s32[]{:S(2)}) async-start(), calls=%async_computation | async-start | bytes 4456448 | tf_op jit(solution)/shard_map/all_gather | solution.py:36
  8.0 116.2 %collective-permute-start.1 = (bf16[512,704]{0,1:T(8,128)(2,1)}, bf16[512,704]{0,1:T(8,128)(2,1)}, u32[]{:S(2)}, u32[]{:S(2)}) collective-permute-start(bf16[512,704]{0,1:T(8,128)(2,1)} %bitcast.40), channel_id=1, source_target_pairs={{0,16},{16,0},{1,17},{17,1},{2,18},{18,2},{3,19},{19,3},{4,20},{20... | collective-permute-start | bytes 2162696 | tf_op jit(solution)/shard_map/ppermute | solution.py:32
  11.0 107.2 %collective-permute-start = (bf16[512,704]{0,1:T(8,128)(2,1)}, bf16[512,704]{0,1:T(8,128)(2,1)}, u32[]{:S(2)}, u32[]{:S(2)}) collective-permute-start(bf16[512,704]{0,1:T(8,128)(2,1)} %bitcast.39), channel_id=1, source_target_pairs={{0,16},{16,0},{1,17},{17,1},{2,18},{18,2},{3,19},{19,3},{4,20},{20... | collective-permute-start | bytes 2162696 | tf_op jit(solution)/shard_map/ppermute | solution.py:31
  63.0 4.3 %copy-start.3 = (bf16[1,512,704]{1,2,0:T(8,128)(2,1)S(1)}, bf16[1,512,704]{1,2,0:T(8,128)(2,1)}, u32[]{:S(2)}) copy-start(bf16[1,512,704]{1,2,0:T(8,128)(2,1)} %param.12) | copy-start | bytes 2162692
  66.0 1.3 copy-start.1
  114.2 3.0 %copy-start.4 = (bf16[1,512,704]{1,2,0:T(8,128)(2,1)S(1)}, bf16[1,512,704]{1,2,0:T(8,128)(2,1)}, u32[]{:S(2)}) copy-start(bf16[1,512,704]{1,2,0:T(8,128)(2,1)} %param.13) | copy-start | bytes 2162692
  117.2 1.6 copy-start.2
  120.9 3.4 %copy-start.5 = (f32[1024,704]{0,1:T(8,128)S(1)}, f32[1024,704]{0,1:T(8,128)}, u32[]{:S(2)}) copy-start(f32[1024,704]{0,1:T(8,128)} %fusion.11) | copy-start | bytes 8650756
  129.3 19.0 %collective-permute-start.3 = (bf16[512,704]{0,1:T(8,128)(2,1)S(1)}, bf16[512,704]{0,1:T(8,128)(2,1)S(1)}, u32[]{:S(2)}, u32[]{:S(2)}) collective-permute-start(bf16[512,704]{0,1:T(8,128)(2,1)S(1)} %convolution_convert_fusion.1), channel_id=1, source_target_pairs={{0,16},{16,0},{1,17},{17,1},{2,18},{18,2},{3,19},{19,3},{4,20},{20... | collective-permute-start | bytes 2162696 | tf_op jit(solution)/shard_map/ppermute | solution.py:75
  131.7 31.3 %collective-permute-start.2 = (bf16[512,704]{0,1:T(8,128)(2,1)S(1)}, bf16[512,704]{0,1:T(8,128)(2,1)S(1)}, u32[]{:S(2)}, u32[]{:S(2)}) collective-permute-start(bf16[512,704]{0,1:T(8,128)(2,1)S(1)} %convolution_convert_fusion.2), channel_id=1, source_target_pairs={{0,16},{16,0},{1,17},{17,1},{2,18},{18,2},{3,19},{19,3},{4,20},{20... | collective-permute-start | bytes 2162696 | tf_op jit(solution)/shard_map/ppermute | solution.py:75
Sparse Core Ops, SparseCore 0:
  9.5 53.4 all-gather.8
  65.1 49.0 all-gather.6

commit v2 on v1

--- a/solution.py
+++ b/solution.py
@@ -32,30 +32,62 @@
         dir_far = lax.ppermute(dir_gate[0], "rep", pairs)
 
     meta = jnp.concatenate([expert_ids.astype(jnp.bfloat16), gate_probs], axis=1).T
-    meta = lax.all_gather(meta, "ep", axis=0, tiled=False)
-    all_tokens = lax.all_gather(tokens, "ep", axis=0, tiled=False)
-    all_query = lax.all_gather(query, "ep", axis=0, tiled=False)
 
-    routed = (meta[:, :top_count].astype(jnp.int32) == me).astype(jnp.float32)
-    gates = jnp.sum(routed * meta[:, top_count:].astype(jnp.float32), axis=1)
-    chosen = jnp.sum(routed, axis=1)
     order = jnp.arange(tok_count, dtype=jnp.int32)
     before = (order[:, None] < order[None, :]).astype(jnp.bfloat16)
-    rank = dot(chosen.astype(jnp.bfloat16), before)
     slots = jnp.arange(capacity, dtype=jnp.float32)
-    match = (rank[:, None, :] == slots[None, :, None]) & (chosen[:, None, :] > 0.5)
-    place = match.astype(jnp.bfloat16)
-    gate_rows = jnp.sum(jnp.where(match, gates[:, None, :], 0.0), axis=2)
 
-    def pick(rows):
-        return lax.dot_general(
-            place, rows, (((2,), (1,)), ((0,), (0,))), preferred_element_type=jnp.float32
+    def pick(all_tokens, all_query, meta):
+        routed = (meta[:, :top_count].astype(jnp.int32) == me).astype(jnp.float32)
+        gates = jnp.sum(
+            routed * meta[:, top_count : 2 * top_count].astype(jnp.float32), axis=1
+        )
+        chosen = jnp.sum(routed, axis=1)
+        rank = dot(chosen.astype(jnp.bfloat16), before)
+        match = (rank[:, None, :] == slots[None, :, None]) & (chosen[:, None, :] > 0.5)
+        place = match.astype(jnp.bfloat16)
+        gate_rows = jnp.sum(jnp.where(match, gates[:, None, :], 0.0), axis=2)
+        picked = [
+            lax.dot_general(
+                place, rows, (((2,), (1,)), ((0,), (0,))), preferred_element_type=jnp.float32
+            )
+            for rows in (all_tokens, all_query)
+        ]
+        token_rows = picked[0].astype(jnp.bfloat16).reshape(-1, model_width)
+        scaled = (gate_rows[:, :, None] * picked[1]).astype(jnp.bfloat16)
+        return token_rows, scaled.reshape(-1, model_width)
+
+    def split(blocks):
+        return (
+            blocks[:, :tok_count],
+            blocks[:, tok_count : 2 * tok_count],
+            blocks[:, 2 * tok_count :, :tok_count],
         )
 
-    token_rows = pick(all_tokens).astype(jnp.bfloat16).reshape(-1, model_width)
-    scaled = (gate_rows[:, :, None] * pick(all_query)).astype(jnp.bfloat16).reshape(-1, model_width)
+    if experts == 16 and reps == 2:
+        meta_rows = -(-2 * top_count // 16) * 16
+        meta = jnp.pad(meta, ((0, meta_rows - 2 * top_count), (0, model_width - tok_count)))
+        block = jnp.concatenate([tokens, query, meta], axis=0)
 
-    pre_act = dot(token_rows, w_gate_up[0])
+        def move(array, target):
+            return lax.ppermute(array, "ep", [(i, target(i)) for i in range(experts)])
+
+        lane = [block] + [move(block, lambda i: (i + 4 * k) % experts) for k in (1, 3, 2)]
+        across = [move(each, lambda i: i ^ 2) for each in lane]
+        near, far = jnp.stack(lane), jnp.stack(across)
+        groups = [
+            [split(near), split(move(near, lambda i: i ^ 1))],
+            [split(far), split(move(far, lambda i: i ^ 1))],
+        ]
+    else:
+        groups = [
+            [[lax.all_gather(each, "ep", axis=0, tiled=False) for each in (tokens, query, meta)]]
+        ]
+    rows = []
+    for group in groups:
+        picked = [pick(*blocks) for blocks in group]
+        rows.append([jnp.concatenate(part, axis=0) for part in zip(*picked)])
+
     if reps == 2:
         half = model_width // 2
         own_at = lax.axis_index("rep") * half
@@ -64,12 +96,20 @@
         def columns(array, at):
             return lax.dynamic_slice_in_dim(array, at, half, axis=1)
 
-        near_tokens, far_tokens = columns(token_rows, own_at), columns(token_rows, far_at)
-        error = dot(columns(scaled, own_at), w_down[0]) + dot(columns(scaled, far_at), w_down_far)
-        tangent = dot(near_tokens, dir_gate[0]) + dot(far_tokens, dir_far)
-        parts = make_factors(
-            pre_act[:, :hidden_width], pre_act[:, hidden_width:], error, tangent
-        )
+        near_tokens, far_tokens, factors = [], [], []
+        for token_rows, scaled in rows:
+            pre_act = dot(token_rows, w_gate_up[0])
+            near_tokens.append(columns(token_rows, own_at))
+            far_tokens.append(columns(token_rows, far_at))
+            error = dot(columns(scaled, own_at), w_down[0]) + dot(
+                columns(scaled, far_at), w_down_far
+            )
+            tangent = dot(near_tokens[-1], dir_gate[0]) + dot(far_tokens[-1], dir_far)
+            factors.append(
+                make_factors(pre_act[:, :hidden_width], pre_act[:, hidden_width:], error, tangent)
+            )
+        near_tokens, far_tokens = jnp.concatenate(near_tokens), jnp.concatenate(far_tokens)
+        parts = [jnp.concatenate(part) for part in zip(*factors)]
         first = ((0,), (0,))
         got = [
             lax.ppermute(dot(far_tokens, part, first).astype(jnp.bfloat16), "rep", pairs)
@@ -79,6 +119,8 @@
         return jnp.concatenate(
             [k + g.astype(jnp.float32) for k, g in zip(kept, got)], axis=1
         )[None]
+    token_rows, scaled = rows[0]
+    pre_act = dot(token_rows, w_gate_up[0])
     error = dot(scaled, lax.all_gather(w_down[0], "rep", axis=0, tiled=True))
     tangent = dot(token_rows, lax.all_gather(dir_gate[0], "rep", axis=0, tiled=True))
     factors = jnp.concatenate(

time: 176 us -> 146 us (0.83)
  blocking collectives: 22.5 us -> 0 us
  between operations: 13.6 us -> 0.28 us
  starting transfers between devices: 5.27 us -> 17.6 us
  waiting for transfers between devices: 103 us -> 94 us
  other arithmetic: 3.53 us -> 9.77 us
  matrix products: 22.8 us -> 20.8 us
  local copies, waits for them, and re-layouts: 5.3 us -> 3.38 us
    all_gather x2 -> x0, waiting for transfers between devices: 72 us -> none  [the longest x1 44.4 us: on_device(): all_tokens = lax.all_gather(tokens, 'ep', axis=0, tiled=False)]
    ppermute x0 -> x9, waiting for transfers between devices: none -> 64.3 us  [move(): return lax.ppermute(array, 'ep', [(i, target(i)) for i in range(experts)])]
    all_gather x1 -> x0, blocking collectives: 22.5 us -> none  [on_device(): meta = lax.all_gather(meta, 'ep', axis=0, tiled=False)]
    ppermute x0 -> x9, starting transfers between devices: none -> 13.4 us  [move(): return lax.ppermute(array, 'ep', [(i, target(i)) for i in range(experts)])]
    another operation x0 -> x3, other arithmetic: none -> 5.54 us  [on_device(): near, far = (jnp.stack(lane), jnp.stack(across))]
    dot_general x2 -> x8, matrix products: 5.94 us -> 2.38 us  [pick(): lax.dot_general(place, rows, (((2,), (1,)), ((0,), (0,))), preferred_elem...]
    unnamed x12 -> x4, local copies, waits for them, and re-layouts: 1.92 us -> 0.01 us
    dot_general x10 -> x18, matrix products: 16.8 us -> 18.4 us  [dot(): lax.dot_general(a, b, (contract, ((), ())), preferred_element_type=jnp.fl...]
  transfers between devices with their start and end apart: 6 -> 13, of which waited for: 4 -> 7; matrix products, arithmetic and copies ran while one was open for 11% -> 14% of each run, Pallas kernels for 0% -> 0%
where the time goes in v2:
time: 146 us
  waiting for transfers between devices  94 us (64%)
  matrix products  20.8 us (14%)
  starting transfers between devices  17.6 us (12%)
  other arithmetic  9.77 us (7%)
  local copies, waits for them, and re-layouts  3.38 us (2%)
    ppermute x9, waiting for transfers between devices, move(): return lax.ppermute(array, 'ep', [(i, target(i)) for i in range(experts)])  64.3 us
    ppermute x2, waiting for transfers between devices, on_device(): lax.ppermute(dot(far_tokens, part, first).astype(jnp.bfloat16), 'rep', pa...  29.7 us
    dot_general x18, matrix products, dot(): lax.dot_general(a, b, (contract, ((), ())), preferred_element_type=jnp.fl...  18.4 us
    ppermute x9, starting transfers between devices, move(): return lax.ppermute(array, 'ep', [(i, target(i)) for i in range(experts)])  13.4 us
    another operation x3, other arithmetic, on_device(): near, far = (jnp.stack(lane), jnp.stack(across))  5.54 us
    broadcast_in_dim x1, local copies, waits for them, and re-layouts, on_device(): jnp.concatenate([k + g.astype(jnp.float32) for k, g in zip(kept, got)], a...  3.37 us
  transfers between devices with their start and end apart: 13, of which 7 were waited for; matrix products, arithmetic and copies ran while one was open for 14% of the time, Pallas kernels for 0%

profile of v2, /device:TPU:0, one launch (start us, length us, event | category | flops | bytes accessed | tf_op | source)
XLA Modules:
  0.0 145.8 jit_solution(14419603939176223546)
XLA Ops:
  1.6 2.0 %fusion.106 = (bf16[1,272,1024]{2,1,0:T(8,128)(2,1)S(1)}, bf16[272,1024]{1,0:T(8,128)(2,1)}) fusion(bf16[12,128]{1,0:T(8,128)(2,1)S(1)} %maximum_bitcast_fusion.1, bf16[128,1024]{1,0:T(8,128)(2,1)} %param.8, bf16[128,1024]{1,0:T(8,128)(2,1)} %param.7), kind=kLoop, calls=%fused_computation.170 | loop fusion | flops 2228224 | bytes 1641472 | tf_op jit(solution)/shard_map/stack | solution.py:77
  3.5 4.0 %collective-permute-start.2 = (bf16[272,1024]{1,0:T(8,128)(2,1)}, bf16[272,1024]{1,0:T(8,128)(2,1)}, u32[]{:S(2)}, u32[]{:S(2)}) collective-permute-start(bf16[272,1024]{1,0:T(8,128)(2,1)} %get-tuple-element.22), channel_id=1, source_target_pairs={{0,8},{1,9},{2,10},{3,11},{4,12},{5,13},{6,14},{7,15},{8,0},{9,1},... | collective-permute-start | bytes 1671176 | tf_op jit(solution)/shard_map/ppermute | solution.py:73
  7.6 1.6 %collective-permute-start = (bf16[272,1024]{1,0:T(8,128)(2,1)}, bf16[272,1024]{1,0:T(8,128)(2,1)}, u32[]{:S(2)}, u32[]{:S(2)}) collective-permute-start(bf16[272,1024]{1,0:T(8,128)(2,1)} %get-tuple-element.22), channel_id=1, source_target_pairs={{0,4},{1,5},{2,6},{3,7},{4,8},{5,9},{6,10},{7,11},{8,12},{9,13},{1... | collective-permute-start | bytes 1671176 | tf_op jit(solution)/shard_map/ppermute | solution.py:73
  9.2 2.2 %collective-permute-start.1 = (bf16[272,1024]{1,0:T(8,128)(2,1)}, bf16[272,1024]{1,0:T(8,128)(2,1)}, u32[]{:S(2)}, u32[]{:S(2)}) collective-permute-start(bf16[272,1024]{1,0:T(8,128)(2,1)} %get-tuple-element.22), channel_id=1, source_target_pairs={{0,12},{1,13},{2,14},{3,15},{4,0},{5,1},{6,2},{7,3},{8,4},{9,5},{1... | collective-permute-start | bytes 1671176 | tf_op jit(solution)/shard_map/ppermute | solution.py:73
  11.4 1.5 %collective-permute-start.4 = (bf16[272,1024]{1,0:T(8,128)(2,1)}, bf16[272,1024]{1,0:T(8,128)(2,1)}, u32[]{:S(2)}, u32[]{:S(2)}) collective-permute-start(bf16[272,1024]{1,0:T(8,128)(2,1)} %get-tuple-element.22), channel_id=1, source_target_pairs={{0,2},{1,3},{2,0},{3,1},{4,6},{5,7},{6,4},{7,5},{8,10},{9,11},{10,... | collective-permute-start | bytes 1671176 | tf_op jit(solution)/shard_map/ppermute | solution.py:73
  12.9 32.3 %collective-permute-done.2 = bf16[272,1024]{1,0:T(8,128)(2,1)} collective-permute-done((bf16[272,1024]{1,0:T(8,128)(2,1)}, bf16[272,1024]{1,0:T(8,128)(2,1)}, u32[]{:S(2)}, u32[]{:S(2)}) %collective-permute-start.2) | collective-permute-done | bytes 557088 | tf_op jit(solution)/shard_map/ppermute | solution.py:73
  45.3 1.9 %collective-permute-start.7 = (bf16[272,1024]{1,0:T(8,128)(2,1)}, bf16[272,1024]{1,0:T(8,128)(2,1)}, u32[]{:S(2)}, u32[]{:S(2)}) collective-permute-start(bf16[272,1024]{1,0:T(8,128)(2,1)} %collective-permute-done.2), channel_id=1, source_target_pairs={{0,2},{1,3},{2,0},{3,1},{4,6},{5,7},{6,4},{7,5},{8,10},{9,11},{10,... | collective-permute-start | bytes 1671176 | tf_op jit(solution)/shard_map/ppermute | solution.py:73
  47.3 1.9 %collective-permute-start.6 = (bf16[272,1024]{1,0:T(8,128)(2,1)}, bf16[272,1024]{1,0:T(8,128)(2,1)}, u32[]{:S(2)}, u32[]{:S(2)}) collective-permute-start(bf16[272,1024]{1,0:T(8,128)(2,1)} %collective-permute-done.1), channel_id=1, source_target_pairs={{0,2},{1,3},{2,0},{3,1},{4,6},{5,7},{6,4},{7,5},{8,10},{9,11},{10,... | collective-permute-start | bytes 1671176 | tf_op jit(solution)/shard_map/ppermute | solution.py:73
  49.2 1.5 %collective-permute-start.10 = (bf16[512,704]{0,1:T(8,128)(2,1)}, bf16[512,704]{0,1:T(8,128)(2,1)}, u32[]{:S(2)}, u32[]{:S(2)}) collective-permute-start(bf16[512,704]{0,1:T(8,128)(2,1)} %bitcast.16), channel_id=1, source_target_pairs={{0,16},{16,0},{1,17},{17,1},{2,18},{18,2},{3,19},{19,3},{4,20},{20... | collective-permute-start | bytes 2162696 | tf_op jit(solution)/shard_map/ppermute | solution.py:32
  50.7 1.7 %pad_maximum_fusion = bf16[4,272,1024]{2,1,0:T(8,128)(2,1)S(1)} fusion(bf16[1,272,1024]{2,1,0:T(8,128)(2,1)} %bitcast.4, bf16[1,272,1024]{2,1,0:T(8,128)(2,1)} %bitcast.3, bf16[1,272,1024]{2,1,0:T(8,128)(2,1)} %bitcast.2, bf16[1,272,1024]{2,1,0:T(8,128)(2,1)S(1)} %get-tuple-element.21), kind=kLoop, calls=%fused_computation.5 | loop fusion | flops 3342336 | bytes 4456448 | tf_op jit(solution)/shard_map/stack | solution.py:77
  53.1 8.1 %collective-permute-done.7 = bf16[272,1024]{1,0:T(8,128)(2,1)} collective-permute-done((bf16[272,1024]{1,0:T(8,128)(2,1)}, bf16[272,1024]{1,0:T(8,128)(2,1)}, u32[]{:S(2)}, u32[]{:S(2)}) %collective-permute-start.7) | collective-permute-done | bytes 557088 | tf_op jit(solution)/shard_map/ppermute | solution.py:73
  61.1 11.9 %collective-permute-done.5 = bf16[272,1024]{1,0:T(8,128)(2,1)} collective-permute-done((bf16[272,1024]{1,0:T(8,128)(2,1)}, bf16[272,1024]{1,0:T(8,128)(2,1)}, u32[]{:S(2)}, u32[]{:S(2)}) %collective-permute-start.5) | collective-permute-done | bytes 557088 | tf_op jit(solution)/shard_map/ppermute | solution.py:73
  73.1 9.4 %collective-permute-done.6 = bf16[272,1024]{1,0:T(8,128)(2,1)} collective-permute-done((bf16[272,1024]{1,0:T(8,128)(2,1)}, bf16[272,1024]{1,0:T(8,128)(2,1)}, u32[]{:S(2)}, u32[]{:S(2)}) %collective-permute-start.6) | collective-permute-done | bytes 557088 | tf_op jit(solution)/shard_map/ppermute | solution.py:73
  82.4 1.8 %pad_maximum_fusion.1 = bf16[4,272,1024]{2,1,0:T(8,128)(2,1)S(1)} fusion(bf16[1,272,1024]{2,1,0:T(8,128)(2,1)} %bitcast.10, bf16[1,272,1024]{2,1,0:T(8,128)(2,1)} %bitcast.9, bf16[1,272,1024]{2,1,0:T(8,128)(2,1)} %bitcast.8, bf16[1,272,1024]{2,1,0:T(8,128)(2,1)} %bitcast.7), kind=kLoop, calls=%fused_computation.6 | loop fusion | flops 3342336 | bytes 4456448 | tf_op jit(solution)/shard_map/stack | solution.py:77
  86.2 2.5 %collective-permute-done.8 = bf16[4,272,1024]{2,1,0:T(8,128)(2,1)S(1)} collective-permute-done((bf16[4,272,1024]{2,1,0:T(8,128)(2,1)S(1)}, bf16[4,272,1024]{2,1,0:T(8,128)(2,1)S(1)}, u32[]{:S(2)}, u32[]{:S(2)}) %collective-permute-start.8) | collective-permute-done | bytes 2228256 | tf_op jit(solution)/shard_map/ppermute | solution.py:73
  89.6 1.7 %fusion.102 = f32[512,704]{0,1:T(8,128)S(1)} fusion(bf16[512,512]{1,0:T(8,128)(2,1)S(1)} %get-tuple-element.18, bf16[1,512,704]{1,2,0:T(8,128)(2,1)} %param.13), kind=kOutput, calls=%fused_computation.166 | convolution fusion | flops 369098752 | bytes 2686976 | tf_op jit(solution)/shard_map/dot_general | solution.py:16
  92.7 1.7 %fusion.100 = f32[512,704]{0,1:T(8,128)S(1)} fusion(bf16[512,512]{1,0:T(8,128)(2,1)S(1)} %get-tuple-element.20, bf16[1,512,704]{1,2,0:T(8,128)(2,1)} %param.13), kind=kOutput, calls=%fused_computation.164 | convolution fusion | flops 369098752 | bytes 2686976 | tf_op jit(solution)/shard_map/dot_general | solution.py:16
  94.4 1.7 %fusion.2 = f32[512,1408]{0,1:T(8,128)S(1)} fusion(bf16[1,1024,1408]{2,1,0:T(8,128)(2,1)S(1)} %copy-done, bf16[256,1024]{1,0:T(8,128)(2,1)S(1)} %bitcast.52, bf16[256,1024]{1,0:T(8,128)(2,1)S(1)} %bitcast.48), kind=kOutput, calls=%fused_computation.3 | convolution fusion | flops 1478492160 | bytes 6815744 | tf_op jit(solution)/shard_map/dot_general | solution.py:16
  96.1 1.7 %convolution_add_fusion.2 = f32[512,704]{0,1:T(8,128)S(1)} fusion(f32[512,704]{0,1:T(8,128)S(1)} %fusion.102, bf16[512,512]{1,0:T(8,128)(2,1)S(1)} %get-tuple-element.17, bf16[512,704]{0,1:T(8,128)(2,1)} %collective-permute-done.10), kind=kOutput, calls=%fused_computation.13 | convolution fusion | flops 369459200 | bytes 4128768 | tf_op jit(solution)/shard_map/dot_general | solution.py:16
  97.8 1.7 %convolution_add_fusion = f32[512,704]{0,1:T(8,128)S(1)} fusion(f32[512,704]{0,1:T(8,128)S(1)} %fusion.100, bf16[512,512]{1,0:T(8,128)(2,1)S(1)} %get-tuple-element.19, bf16[512,704]{0,1:T(8,128)(2,1)} %collective-permute-done.10), kind=kOutput, calls=%fused_computation.11 | convolution fusion | flops 369459200 | bytes 4128768 | tf_op jit(solution)/shard_map/dot_general | solution.py:16
  100.4 1.7 %fusion = f32[512,1408]{0,1:T(8,128)S(1)} fusion(bf16[1,1024,1408]{2,1,0:T(8,128)(2,1)S(1)} %copy-done, bf16[256,1024]{1,0:T(8,128)(2,1)S(1)} %bitcast.50, bf16[256,1024]{1,0:T(8,128)(2,1)S(1)} %bitcast.46), kind=kOutput, calls=%fused_computation.1 | convolution fusion | flops 1478492160 | bytes 6815744 | tf_op jit(solution)/shard_map/dot_general | solution.py:16
  102.1 1.4 fusion.8
  103.5 1.5 %fusion.15 = (bf16[512,704]{0,1:T(8,128)(2,1)S(1)}, bf16[512,704]{0,1:T(8,128)(2,1)S(1)}) fusion(f32[512,1408]{0,1:T(8,128)S(1)} %fusion, f32[512,704]{0,1:T(8,128)S(1)} %convolution_add_fusion, f32[512,704]{0,1:T(8,128)S(1)} %fusion.39, bf16[512,704]{0,1:T(8,128)(2,1)S(1)} %collective-permute-done.9, s32[]{:T(128)S(6)} %select_n.28, ...), kind=kOutput, calls=%fused_computation.26 | convolution fusion | flops 377356288 | bytes 8978436 | tf_op jit(solution)/shard_map/dot_general | solution.py:16
  105.0 0.9 convolution_convert_fusion.1
  105.9 1.3 collective-permute-start.11
  107.3 0.9 convolution_convert_fusion
  109.0 16.0 %collective-permute-done.11 = bf16[512,704]{0,1:T(8,128)(2,1)S(1)} collective-permute-done((bf16[512,704]{0,1:T(8,128)(2,1)S(1)}, bf16[512,704]{0,1:T(8,128)(2,1)S(1)}, u32[]{:S(2)}, u32[]{:S(2)}) %collective-permute-start.11) | collective-permute-done | bytes 720928 | tf_op jit(solution)/shard_map/ppermute | solution.py:115
  125.0 0.9 convert_add_fusion.1
  125.9 13.7 %collective-permute-done.12 = bf16[512,704]{0,1:T(8,128)(2,1)S(1)} collective-permute-done((bf16[512,704]{0,1:T(8,128)(2,1)S(1)}, bf16[512,704]{0,1:T(8,128)(2,1)S(1)}, u32[]{:S(2)}, u32[]{:S(2)}) %collective-permute-start.12) | collective-permute-done | bytes 720928 | tf_op jit(solution)/shard_map/ppermute | solution.py:115
  139.6 0.9 convert_add_fusion
  140.5 1.8 %maximum_bitcast_fusion = f32[1,512,1408]{1,2,0:T(8,128)} fusion(f32[512,704]{0,1:T(8,128)S(1)} %convert_add_fusion, f32[512,704]{0,1:T(8,128)S(1)} %convert_add_fusion.1), kind=kLoop, calls=%fused_computation | loop fusion | flops 720896 | bytes 5767168 | tf_op jit(solution)/shard_map/broadcast_in_dim | solution.py:119
  142.4 3.4 %copy.12 = f32[1,512,1408]{2,1,0:T(8,128)} copy(f32[1,512,1408]{1,2,0:T(8,128)} %maximum_bitcast_fusion) | data formatting | bytes 5767168 | tf_op jit(solution)/shard_map/broadcast_in_dim | solution.py:119
  (44 shorter events, 8.2 us)
Async XLA Ops:
  0.0 94.4 %copy-start = (bf16[1,1024,1408]{2,1,0:T(8,128)(2,1)S(1)}, bf16[1,1024,1408]{2,1,0:T(8,128)(2,1)}, u32[]{:S(2)}) copy-start(bf16[1,1024,1408]{2,1,0:T(8,128)(2,1)} %param.11) | copy-start | bytes 8650756
  3.5 41.7 %collective-permute-start.2 = (bf16[272,1024]{1,0:T(8,128)(2,1)}, bf16[272,1024]{1,0:T(8,128)(2,1)}, u32[]{:S(2)}, u32[]{:S(2)}) collective-permute-start(bf16[272,1024]{1,0:T(8,128)(2,1)} %get-tuple-element.22), channel_id=1, source_target_pairs={{0,8},{1,9},{2,10},{3,11},{4,12},{5,13},{6,14},{7,15},{8,0},{9,1},... | collective-permute-start | bytes 1671176 | tf_op jit(solution)/shard_map/ppermute | solution.py:73
  7.6 39.6 %collective-permute-start = (bf16[272,1024]{1,0:T(8,128)(2,1)}, bf16[272,1024]{1,0:T(8,128)(2,1)}, u32[]{:S(2)}, u32[]{:S(2)}) collective-permute-start(bf16[272,1024]{1,0:T(8,128)(2,1)} %get-tuple-element.22), channel_id=1, source_target_pairs={{0,4},{1,5},{2,6},{3,7},{4,8},{5,9},{6,10},{7,11},{8,12},{9,13},{1... | collective-permute-start | bytes 1671176 | tf_op jit(solution)/shard_map/ppermute | solution.py:73
  9.2 38.1 %collective-permute-start.1 = (bf16[272,1024]{1,0:T(8,128)(2,1)}, bf16[272,1024]{1,0:T(8,128)(2,1)}, u32[]{:S(2)}, u32[]{:S(2)}) collective-permute-start(bf16[272,1024]{1,0:T(8,128)(2,1)} %get-tuple-element.22), channel_id=1, source_target_pairs={{0,12},{1,13},{2,14},{3,15},{4,0},{5,1},{6,2},{7,3},{8,4},{9,5},{1... | collective-permute-start | bytes 1671176 | tf_op jit(solution)/shard_map/ppermute | solution.py:73
  11.4 41.0 %collective-permute-start.4 = (bf16[272,1024]{1,0:T(8,128)(2,1)}, bf16[272,1024]{1,0:T(8,128)(2,1)}, u32[]{:S(2)}, u32[]{:S(2)}) collective-permute-start(bf16[272,1024]{1,0:T(8,128)(2,1)} %get-tuple-element.22), channel_id=1, source_target_pairs={{0,2},{1,3},{2,0},{3,1},{4,6},{5,7},{6,4},{7,5},{8,10},{9,11},{10,... | collective-permute-start | bytes 1671176 | tf_op jit(solution)/shard_map/ppermute | solution.py:73
  45.3 15.9 %collective-permute-start.7 = (bf16[272,1024]{1,0:T(8,128)(2,1)}, bf16[272,1024]{1,0:T(8,128)(2,1)}, u32[]{:S(2)}, u32[]{:S(2)}) collective-permute-start(bf16[272,1024]{1,0:T(8,128)(2,1)} %collective-permute-done.2), channel_id=1, source_target_pairs={{0,2},{1,3},{2,0},{3,1},{4,6},{5,7},{6,4},{7,5},{8,10},{9,11},{10,... | collective-permute-start | bytes 1671176 | tf_op jit(solution)/shard_map/ppermute | solution.py:73
  47.1 25.9 %collective-permute-start.5 = (bf16[272,1024]{1,0:T(8,128)(2,1)}, bf16[272,1024]{1,0:T(8,128)(2,1)}, u32[]{:S(2)}, u32[]{:S(2)}) collective-permute-start(bf16[272,1024]{1,0:T(8,128)(2,1)} %collective-permute-done), channel_id=1, source_target_pairs={{0,2},{1,3},{2,0},{3,1},{4,6},{5,7},{6,4},{7,5},{8,10},{9,11},{10,... | collective-permute-start | bytes 1671176 | tf_op jit(solution)/shard_map/ppermute | solution.py:73
  47.3 35.1 %collective-permute-start.6 = (bf16[272,1024]{1,0:T(8,128)(2,1)}, bf16[272,1024]{1,0:T(8,128)(2,1)}, u32[]{:S(2)}, u32[]{:S(2)}) collective-permute-start(bf16[272,1024]{1,0:T(8,128)(2,1)} %collective-permute-done.1), channel_id=1, source_target_pairs={{0,2},{1,3},{2,0},{3,1},{4,6},{5,7},{6,4},{7,5},{8,10},{9,11},{10,... | collective-permute-start | bytes 1671176 | tf_op jit(solution)/shard_map/ppermute | solution.py:73
  49.2 46.9 %collective-permute-start.10 = (bf16[512,704]{0,1:T(8,128)(2,1)}, bf16[512,704]{0,1:T(8,128)(2,1)}, u32[]{:S(2)}, u32[]{:S(2)}) collective-permute-start(bf16[512,704]{0,1:T(8,128)(2,1)} %bitcast.16), channel_id=1, source_target_pairs={{0,16},{16,0},{1,17},{17,1},{2,18},{18,2},{3,19},{19,3},{4,20},{20... | collective-permute-start | bytes 2162696 | tf_op jit(solution)/shard_map/ppermute | solution.py:32
  50.7 1.8 %copy-start.1 = (bf16[1,512,704]{1,2,0:T(8,128)(2,1)S(1)}, bf16[1,512,704]{1,2,0:T(8,128)(2,1)}, u32[]{:S(2)}) copy-start(bf16[1,512,704]{1,2,0:T(8,128)(2,1)} %param.12) | copy-start | bytes 2162692
  52.5 49.7 %collective-permute-start.9 = (bf16[512,704]{0,1:T(8,128)(2,1)S(1)}, bf16[512,704]{0,1:T(8,128)(2,1)S(1)}, u32[]{:S(2)}, u32[]{:S(2)}) collective-permute-start(bf16[512,704]{0,1:T(8,128)(2,1)S(1)} %bitcast.44), channel_id=1, source_target_pairs={{0,16},{16,0},{1,17},{17,1},{2,18},{18,2},{3,19},{19,3},{4,20},{20... | collective-permute-start | bytes 2162696 | tf_op jit(solution)/shard_map/ppermute | solution.py:31
  61.1 25.0 %collective-permute-start.3 = (bf16[4,272,1024]{2,1,0:T(8,128)(2,1)S(1)}, bf16[4,272,1024]{2,1,0:T(8,128)(2,1)S(1)}, u32[]{:S(2)}, u32[]{:S(2)}) collective-permute-start(bf16[4,272,1024]{2,1,0:T(8,128)(2,1)S(1)} %pad_maximum_fusion), channel_id=1, source_target_pairs={{0,1},{1,0},{2,3},{3,2},{4,5},{5,4},{6,7},{7,6},{8,9},{9,8},{10,11... | collective-permute-start | bytes 6684680 | tf_op jit(solution)/shard_map/ppermute | solution.py:73
  84.3 4.4 %collective-permute-start.8 = (bf16[4,272,1024]{2,1,0:T(8,128)(2,1)S(1)}, bf16[4,272,1024]{2,1,0:T(8,128)(2,1)S(1)}, u32[]{:S(2)}, u32[]{:S(2)}) collective-permute-start(bf16[4,272,1024]{2,1,0:T(8,128)(2,1)S(1)} %pad_maximum_fusion.1), channel_id=1, source_target_pairs={{0,1},{1,0},{2,3},{3,2},{4,5},{5,4},{6,7},{7,6},{8,9},{9,8},{10,11... | collective-permute-start | bytes 6684680 | tf_op jit(solution)/shard_map/ppermute | solution.py:73
  105.9 19.0 %collective-permute-start.11 = (bf16[512,704]{0,1:T(8,128)(2,1)S(1)}, bf16[512,704]{0,1:T(8,128)(2,1)S(1)}, u32[]{:S(2)}, u32[]{:S(2)}) collective-permute-start(bf16[512,704]{0,1:T(8,128)(2,1)S(1)} %convolution_convert_fusion.1), channel_id=1, source_target_pairs={{0,16},{16,0},{1,17},{17,1},{2,18},{18,2},{3,19},{19,3},{4,20},{20... | collective-permute-start | bytes 2162696 | tf_op jit(solution)/shard_map/ppermute | solution.py:115
  108.2 31.5 %collective-permute-start.12 = (bf16[512,704]{0,1:T(8,128)(2,1)S(1)}, bf16[512,704]{0,1:T(8,128)(2,1)S(1)}, u32[]{:S(2)}, u32[]{:S(2)}) collective-permute-start(bf16[512,704]{0,1:T(8,128)(2,1)S(1)} %convolution_convert_fusion), channel_id=1, source_target_pairs={{0,16},{16,0},{1,17},{17,1},{2,18},{18,2},{3,19},{19,3},{4,20},{20... | collective-permute-start | bytes 2162696 | tf_op jit(solution)/shard_map/ppermute | solution.py:115

commit v3 on v2

--- a/solution.py
+++ b/solution.py
@@ -72,8 +72,11 @@
         def move(array, target):
             return lax.ppermute(array, "ep", [(i, target(i)) for i in range(experts)])
 
-        lane = [block] + [move(block, lambda i: (i + 4 * k) % experts) for k in (1, 3, 2)]
-        across = [move(each, lambda i: i ^ 2) for each in lane]
+        lane, across = [block], [move(block, lambda i: i ^ 2)]
+        for k in (1, 3, 2):
+            sent = block if k == 1 else block + lane[-1][-1:, -1:]
+            lane.append(move(sent, lambda i: (i + 4 * k) % experts))
+            across.append(move(lane[-1], lambda i: i ^ 2))
         near, far = jnp.stack(lane), jnp.stack(across)
         groups = [
             [split(near), split(move(near, lambda i: i ^ 1))],

time: 146 us -> 154 us (1.055)
  waiting for transfers between devices: 94 us -> 99.6 us
  starting transfers between devices: 17.6 us -> 14.2 us
  local copies, waits for them, and re-layouts: 3.38 us -> 6.08 us
  other arithmetic: 9.77 us -> 12.4 us
    ppermute x9, waiting for transfers between devices: 64.3 us -> 69.9 us  [move(): return lax.ppermute(array, 'ep', [(i, target(i)) for i in range(experts)])]
    ppermute x9, starting transfers between devices: 13.4 us -> 9.95 us  [move(): return lax.ppermute(array, 'ep', [(i, target(i)) for i in range(experts)])]
    slice x0 -> x2, local copies, waits for them, and re-layouts: none -> 2.69 us  [on_device(): sent = block if k == 1 else block + lane[-1][-1:, -1:]]
    concatenate x0 -> x1, other arithmetic: none -> 1.88 us  [on_device(): block = jnp.concatenate([tokens, query, meta], axis=0)]
  transfers between devices with their start and end apart: 13 -> 13, of which waited for: 7 -> 8; matrix products, arithmetic and copies ran while one was open for 14% -> 13% of each run, Pallas kernels for 0% -> 0%
where the time goes in v3:
time: 154 us; the launch traced here: 153 us
  waiting for transfers between devices  99.6 us (65%)
  matrix products  20.8 us (14%)
  starting transfers between devices  14.2 us (9%)
  other arithmetic  12.4 us (8%)
  local copies, waits for them, and re-layouts  6.08 us (4%)
    ppermute x9, waiting for transfers between devices, move(): return lax.ppermute(array, 'ep', [(i, target(i)) for i in range(experts)])  69.9 us
    ppermute x2, waiting for transfers between devices, on_device(): lax.ppermute(dot(far_tokens, part, first).astype(jnp.bfloat16), 'rep', pa...  29.7 us
    dot_general x18, matrix products, dot(): lax.dot_general(a, b, (contract, ((), ())), preferred_element_type=jnp.fl...  18.4 us
    ppermute x9, starting transfers between devices, move(): return lax.ppermute(array, 'ep', [(i, target(i)) for i in range(experts)])  9.95 us
    another operation x3, other arithmetic, on_device(): near, far = (jnp.stack(lane), jnp.stack(across))  5.43 us
    broadcast_in_dim x1, local copies, waits for them, and re-layouts, on_device(): jnp.concatenate([k + g.astype(jnp.float32) for k, g in zip(kept, got)], a...  3.37 us
  transfers between devices with their start and end apart: 13, of which 8 were waited for; matrix products, arithmetic and copies ran while one was open for 13% of the time, Pallas kernels for 0%

profile of v3, /device:TPU:0, one launch (start us, length us, event | category | flops | bytes accessed | tf_op | source)
XLA Modules:
  0.0 153.3 jit_solution(14122616882880532375)
XLA Ops:
  1.6 1.9 %fusion.35 = bf16[272,1024]{1,0:T(8,128)(2,1)} fusion(bf16[12,128]{1,0:T(8,128)(2,1)S(1)} %maximum_bitcast_fusion.1, bf16[128,1024]{1,0:T(8,128)(2,1)} %param.8, bf16[128,1024]{1,0:T(8,128)(2,1)} %param.7), kind=kLoop, calls=%fused_computation.85 | loop fusion | flops 2228224 | bytes 1084416 | tf_op jit(solution)/shard_map/concatenate | solution.py:70
  3.5 3.0 %collective-permute-start = (bf16[272,1024]{1,0:T(8,128)(2,1)}, bf16[272,1024]{1,0:T(8,128)(2,1)}, u32[]{:S(2)}, u32[]{:S(2)}) collective-permute-start(bf16[272,1024]{1,0:T(8,128)(2,1)} %fusion.35), channel_id=1, source_target_pairs={{0,4},{1,5},{2,6},{3,7},{4,8},{5,9},{6,10},{7,11},{8,12},{9,13},{1... | collective-permute-start | bytes 1671176 | tf_op jit(solution)/shard_map/ppermute | solution.py:73
  6.6 15.0 %collective-permute-done = bf16[272,1024]{1,0:T(8,128)(2,1)} collective-permute-done((bf16[272,1024]{1,0:T(8,128)(2,1)}, bf16[272,1024]{1,0:T(8,128)(2,1)}, u32[]{:S(2)}, u32[]{:S(2)}) %collective-permute-start) | collective-permute-done | bytes 557088 | tf_op jit(solution)/shard_map/ppermute | solution.py:73
  21.5 1.3 slice.100
  22.9 1.9 %fusion.106 = (bf16[1,272,1024]{2,1,0:T(8,128)(2,1)S(1)}, bf16[272,1024]{1,0:T(8,128)(2,1)S(1)}) fusion(bf16[12,128]{1,0:T(8,128)(2,1)S(1)} %maximum_bitcast_fusion.1, bf16[128,1024]{1,0:T(8,128)(2,1)} %param.8, bf16[128,1024]{1,0:T(8,128)(2,1)} %param.7, bf16[]{:T(256)} %bitcast.3), kind=kLoop, calls=%fused_computation.172 | loop fusion | flops 3063808 | bytes 1641474 | tf_op jit(solution)/shard_map/stack | solution.py:80
  24.7 1.8 %collective-permute-start.1 = (bf16[272,1024]{1,0:T(8,128)(2,1)S(1)}, bf16[272,1024]{1,0:T(8,128)(2,1)}, u32[]{:S(2)}, u32[]{:S(2)}) collective-permute-start(bf16[272,1024]{1,0:T(8,128)(2,1)S(1)} %get-tuple-element.22), channel_id=1, source_target_pairs={{0,12},{1,13},{2,14},{3,15},{4,0},{5,1},{6,2},{7,3},{8,4},{9,5},{1... | collective-permute-start | bytes 1671176 | tf_op jit(solution)/shard_map/ppermute | solution.py:73
  26.5 12.2 %collective-permute-done.1 = bf16[272,1024]{1,0:T(8,128)(2,1)} collective-permute-done((bf16[272,1024]{1,0:T(8,128)(2,1)S(1)}, bf16[272,1024]{1,0:T(8,128)(2,1)}, u32[]{:S(2)}, u32[]{:S(2)}) %collective-permute-start.1) | collective-permute-done | bytes 557088 | tf_op jit(solution)/shard_map/ppermute | solution.py:73
  38.7 1.3 slice.101
  41.3 1.5 collective-permute-start.4
  43.4 1.5 collective-permute-start.6
  44.9 21.9 %collective-permute-done.2 = bf16[272,1024]{1,0:T(8,128)(2,1)} collective-permute-done((bf16[272,1024]{1,0:T(8,128)(2,1)S(1)}, bf16[272,1024]{1,0:T(8,128)(2,1)}, u32[]{:S(2)}, u32[]{:S(2)}) %collective-permute-start.2) | collective-permute-done | bytes 557088 | tf_op jit(solution)/shard_map/ppermute | solution.py:73
  66.7 1.0 collective-permute-start.7
  67.8 1.5 collective-permute-start.10
  69.3 1.7 %pad_maximum_fusion = bf16[4,272,1024]{2,1,0:T(8,128)(2,1)S(1)} fusion(bf16[1,272,1024]{2,1,0:T(8,128)(2,1)} %bitcast.6, bf16[1,272,1024]{2,1,0:T(8,128)(2,1)} %bitcast.4, bf16[1,272,1024]{2,1,0:T(8,128)(2,1)} %bitcast.2, bf16[1,272,1024]{2,1,0:T(8,128)(2,1)S(1)} %get-tuple-element.21), kind=kLoop, calls=%fused_computation.5 | loop fusion | flops 3342336 | bytes 4456448 | tf_op jit(solution)/shard_map/stack | solution.py:80
  71.7 9.4 %collective-permute-done.6 = bf16[272,1024]{1,0:T(8,128)(2,1)} collective-permute-done((bf16[272,1024]{1,0:T(8,128)(2,1)}, bf16[272,1024]{1,0:T(8,128)(2,1)}, u32[]{:S(2)}, u32[]{:S(2)}) %collective-permute-start.6) | collective-permute-done | bytes 557088 | tf_op jit(solution)/shard_map/ppermute | solution.py:73
  81.1 8.9 %collective-permute-done.7 = bf16[272,1024]{1,0:T(8,128)(2,1)} collective-permute-done((bf16[272,1024]{1,0:T(8,128)(2,1)}, bf16[272,1024]{1,0:T(8,128)(2,1)}, u32[]{:S(2)}, u32[]{:S(2)}) %collective-permute-start.7) | collective-permute-done | bytes 557088 | tf_op jit(solution)/shard_map/ppermute | solution.py:73
  90.0 1.8 %pad_maximum_fusion.1 = bf16[4,272,1024]{2,1,0:T(8,128)(2,1)S(1)} fusion(bf16[1,272,1024]{2,1,0:T(8,128)(2,1)} %bitcast.12, bf16[1,272,1024]{2,1,0:T(8,128)(2,1)} %bitcast.11, bf16[1,272,1024]{2,1,0:T(8,128)(2,1)} %bitcast.10, bf16[1,272,1024]{2,1,0:T(8,128)(2,1)} %bitcast.9), kind=kLoop, calls=%fused_computation.6 | loop fusion | flops 3342336 | bytes 4456448 | tf_op jit(solution)/shard_map/stack | solution.py:80
  93.7 2.5 %collective-permute-done.8 = bf16[4,272,1024]{2,1,0:T(8,128)(2,1)S(1)} collective-permute-done((bf16[4,272,1024]{2,1,0:T(8,128)(2,1)S(1)}, bf16[4,272,1024]{2,1,0:T(8,128)(2,1)S(1)}, u32[]{:S(2)}, u32[]{:S(2)}) %collective-permute-start.8) | collective-permute-done | bytes 2228256 | tf_op jit(solution)/shard_map/ppermute | solution.py:73
  97.1 1.7 %fusion.102 = f32[512,704]{0,1:T(8,128)S(1)} fusion(bf16[512,512]{1,0:T(8,128)(2,1)S(1)} %get-tuple-element.18, bf16[1,512,704]{1,2,0:T(8,128)(2,1)} %param.13), kind=kOutput, calls=%fused_computation.168 | convolution fusion | flops 369098752 | bytes 2686976 | tf_op jit(solution)/shard_map/dot_general | solution.py:16
  100.2 1.7 %fusion.100 = f32[512,704]{0,1:T(8,128)S(1)} fusion(bf16[512,512]{1,0:T(8,128)(2,1)S(1)} %get-tuple-element.20, bf16[1,512,704]{1,2,0:T(8,128)(2,1)} %param.13), kind=kOutput, calls=%fused_computation.166 | convolution fusion | flops 369098752 | bytes 2686976 | tf_op jit(solution)/shard_map/dot_general | solution.py:16
  101.9 1.7 %fusion.2 = f32[512,1408]{0,1:T(8,128)S(1)} fusion(bf16[1,1024,1408]{2,1,0:T(8,128)(2,1)S(1)} %copy-done, bf16[256,1024]{1,0:T(8,128)(2,1)S(1)} %bitcast.54, bf16[256,1024]{1,0:T(8,128)(2,1)S(1)} %bitcast.50), kind=kOutput, calls=%fused_computation.3 | convolution fusion | flops 1478492160 | bytes 6815744 | tf_op jit(solution)/shard_map/dot_general | solution.py:16
  103.7 1.7 %convolution_add_fusion.2 = f32[512,704]{0,1:T(8,128)S(1)} fusion(f32[512,704]{0,1:T(8,128)S(1)} %fusion.102, bf16[512,512]{1,0:T(8,128)(2,1)S(1)} %get-tuple-element.17, bf16[512,704]{0,1:T(8,128)(2,1)} %collective-permute-done.10), kind=kOutput, calls=%fused_computation.13 | convolution fusion | flops 369459200 | bytes 4128768 | tf_op jit(solution)/shard_map/dot_general | solution.py:16
  105.4 1.7 %convolution_add_fusion = f32[512,704]{0,1:T(8,128)S(1)} fusion(f32[512,704]{0,1:T(8,128)S(1)} %fusion.100, bf16[512,512]{1,0:T(8,128)(2,1)S(1)} %get-tuple-element.19, bf16[512,704]{0,1:T(8,128)(2,1)} %collective-permute-done.10), kind=kOutput, calls=%fused_computation.11 | convolution fusion | flops 369459200 | bytes 4128768 | tf_op jit(solution)/shard_map/dot_general | solution.py:16
  108.0 1.7 %fusion = f32[512,1408]{0,1:T(8,128)S(1)} fusion(bf16[1,1024,1408]{2,1,0:T(8,128)(2,1)S(1)} %copy-done, bf16[256,1024]{1,0:T(8,128)(2,1)S(1)} %bitcast.52, bf16[256,1024]{1,0:T(8,128)(2,1)S(1)} %bitcast.48), kind=kOutput, calls=%fused_computation.1 | convolution fusion | flops 1478492160 | bytes 6815744 | tf_op jit(solution)/shard_map/dot_general | solution.py:16
  109.7 1.4 fusion.8
  111.1 1.5 fusion.15
  112.6 0.9 convolution_convert_fusion.1
  113.5 1.3 collective-permute-start.11
  116.6 16.0 %collective-permute-done.11 = bf16[512,704]{0,1:T(8,128)(2,1)S(1)} collective-permute-done((bf16[512,704]{0,1:T(8,128)(2,1)S(1)}, bf16[512,704]{0,1:T(8,128)(2,1)S(1)}, u32[]{:S(2)}, u32[]{:S(2)}) %collective-permute-start.11) | collective-permute-done | bytes 720928 | tf_op jit(solution)/shard_map/ppermute | solution.py:118
  133.5 13.7 %collective-permute-done.12 = bf16[512,704]{0,1:T(8,128)(2,1)S(1)} collective-permute-done((bf16[512,704]{0,1:T(8,128)(2,1)S(1)}, bf16[512,704]{0,1:T(8,128)(2,1)S(1)}, u32[]{:S(2)}, u32[]{:S(2)}) %collective-permute-start.12) | collective-permute-done | bytes 720928 | tf_op jit(solution)/shard_map/ppermute | solution.py:118
  148.1 1.8 %maximum_bitcast_fusion = f32[1,512,1408]{1,2,0:T(8,128)} fusion(f32[512,704]{0,1:T(8,128)S(1)} %convert_add_fusion, f32[512,704]{0,1:T(8,128)S(1)} %convert_add_fusion.1), kind=kLoop, calls=%fused_computation | loop fusion | flops 720896 | bytes 5767168 | tf_op jit(solution)/shard_map/broadcast_in_dim | solution.py:122
  150.0 3.4 %copy.12 = f32[1,512,1408]{2,1,0:T(8,128)} copy(f32[1,512,1408]{1,2,0:T(8,128)} %maximum_bitcast_fusion) | data formatting | bytes 5767168 | tf_op jit(solution)/shard_map/broadcast_in_dim | solution.py:122
  (52 shorter events, 12.6 us)
Async XLA Ops:
  0.0 101.9 %copy-start = (bf16[1,1024,1408]{2,1,0:T(8,128)(2,1)S(1)}, bf16[1,1024,1408]{2,1,0:T(8,128)(2,1)}, u32[]{:S(2)}) copy-start(bf16[1,1024,1408]{2,1,0:T(8,128)(2,1)} %param.11) | copy-start | bytes 8650756
  0.0 40.0 %copy-start.3 = (bf16[128,1024]{1,0:T(8,128)(2,1)S(1)}, bf16[128,1024]{1,0:T(8,128)(2,1)}, u32[]{:S(2)}) copy-start(bf16[128,1024]{1,0:T(8,128)(2,1)} %param.7) | copy-start | bytes 786436
  0.0 40.0 %copy-start.2 = (bf16[128,1024]{1,0:T(8,128)(2,1)S(1)}, bf16[128,1024]{1,0:T(8,128)(2,1)}, u32[]{:S(2)}) copy-start(bf16[128,1024]{1,0:T(8,128)(2,1)} %param.8) | copy-start | bytes 786436
  3.5 18.0 %collective-permute-start = (bf16[272,1024]{1,0:T(8,128)(2,1)}, bf16[272,1024]{1,0:T(8,128)(2,1)}, u32[]{:S(2)}, u32[]{:S(2)}) collective-permute-start(bf16[272,1024]{1,0:T(8,128)(2,1)} %fusion.35), channel_id=1, source_target_pairs={{0,4},{1,5},{2,6},{3,7},{4,8},{5,9},{6,10},{7,11},{8,12},{9,13},{1... | collective-permute-start | bytes 1671176 | tf_op jit(solution)/shard_map/ppermute | solution.py:73
  24.7 14.0 %collective-permute-start.1 = (bf16[272,1024]{1,0:T(8,128)(2,1)S(1)}, bf16[272,1024]{1,0:T(8,128)(2,1)}, u32[]{:S(2)}, u32[]{:S(2)}) collective-permute-start(bf16[272,1024]{1,0:T(8,128)(2,1)S(1)} %get-tuple-element.22), channel_id=1, source_target_pairs={{0,12},{1,13},{2,14},{3,15},{4,0},{5,1},{6,2},{7,3},{8,4},{9,5},{1... | collective-permute-start | bytes 1671176 | tf_op jit(solution)/shard_map/ppermute | solution.py:73
  40.8 25.9 %collective-permute-start.2 = (bf16[272,1024]{1,0:T(8,128)(2,1)S(1)}, bf16[272,1024]{1,0:T(8,128)(2,1)}, u32[]{:S(2)}, u32[]{:S(2)}) collective-permute-start(bf16[272,1024]{1,0:T(8,128)(2,1)S(1)} %broadcast_add_fusion), channel_id=1, source_target_pairs={{0,8},{1,9},{2,10},{3,11},{4,12},{5,13},{6,14},{7,15},{8,0},{9,1},... | collective-permute-start | bytes 1671176 | tf_op jit(solution)/shard_map/ppermute | solution.py:73
  41.3 29.7 %collective-permute-start.4 = (bf16[272,1024]{1,0:T(8,128)(2,1)}, bf16[272,1024]{1,0:T(8,128)(2,1)}, u32[]{:S(2)}, u32[]{:S(2)}) collective-permute-start(bf16[272,1024]{1,0:T(8,128)(2,1)} %fusion.35), channel_id=1, source_target_pairs={{0,2},{1,3},{2,0},{3,1},{4,6},{5,7},{6,4},{7,5},{8,10},{9,11},{10,... | collective-permute-start | bytes 1671176 | tf_op jit(solution)/shard_map/ppermute | solution.py:73
  42.8 28.8 %collective-permute-start.5 = (bf16[272,1024]{1,0:T(8,128)(2,1)}, bf16[272,1024]{1,0:T(8,128)(2,1)}, u32[]{:S(2)}, u32[]{:S(2)}) collective-permute-start(bf16[272,1024]{1,0:T(8,128)(2,1)} %collective-permute-done), channel_id=1, source_target_pairs={{0,2},{1,3},{2,0},{3,1},{4,6},{5,7},{6,4},{7,5},{8,10},{9,11},{10,... | collective-permute-start | bytes 1671176 | tf_op jit(solution)/shard_map/ppermute | solution.py:73
  43.4 37.7 %collective-permute-start.6 = (bf16[272,1024]{1,0:T(8,128)(2,1)}, bf16[272,1024]{1,0:T(8,128)(2,1)}, u32[]{:S(2)}, u32[]{:S(2)}) collective-permute-start(bf16[272,1024]{1,0:T(8,128)(2,1)} %collective-permute-done.1), channel_id=1, source_target_pairs={{0,2},{1,3},{2,0},{3,1},{4,6},{5,7},{6,4},{7,5},{8,10},{9,11},{10,... | collective-permute-start | bytes 1671176 | tf_op jit(solution)/shard_map/ppermute | solution.py:73
  66.7 23.3 %collective-permute-start.7 = (bf16[272,1024]{1,0:T(8,128)(2,1)}, bf16[272,1024]{1,0:T(8,128)(2,1)}, u32[]{:S(2)}, u32[]{:S(2)}) collective-permute-start(bf16[272,1024]{1,0:T(8,128)(2,1)} %collective-permute-done.2), channel_id=1, source_target_pairs={{0,2},{1,3},{2,0},{3,1},{4,6},{5,7},{6,4},{7,5},{8,10},{9,11},{10,... | collective-permute-start | bytes 1671176 | tf_op jit(solution)/shard_map/ppermute | solution.py:73
  67.8 35.9 %collective-permute-start.10 = (bf16[512,704]{0,1:T(8,128)(2,1)}, bf16[512,704]{0,1:T(8,128)(2,1)}, u32[]{:S(2)}, u32[]{:S(2)}) collective-permute-start(bf16[512,704]{0,1:T(8,128)(2,1)} %bitcast.18), channel_id=1, source_target_pairs={{0,16},{16,0},{1,17},{17,1},{2,18},{18,2},{3,19},{19,3},{4,20},{20... | collective-permute-start | bytes 2162696 | tf_op jit(solution)/shard_map/ppermute | solution.py:32
  69.3 1.8 %copy-start.1 = (bf16[1,512,704]{1,2,0:T(8,128)(2,1)S(1)}, bf16[1,512,704]{1,2,0:T(8,128)(2,1)}, u32[]{:S(2)}) copy-start(bf16[1,512,704]{1,2,0:T(8,128)(2,1)} %param.12) | copy-start | bytes 2162692
  71.1 38.6 %collective-permute-start.9 = (bf16[512,704]{0,1:T(8,128)(2,1)S(1)}, bf16[512,704]{0,1:T(8,128)(2,1)S(1)}, u32[]{:S(2)}, u32[]{:S(2)}) collective-permute-start(bf16[512,704]{0,1:T(8,128)(2,1)S(1)} %bitcast.46), channel_id=1, source_target_pairs={{0,16},{16,0},{1,17},{17,1},{2,18},{18,2},{3,19},{19,3},{4,20},{20... | collective-permute-start | bytes 2162696 | tf_op jit(solution)/shard_map/ppermute | solution.py:31
  71.7 22.1 %collective-permute-start.3 = (bf16[4,272,1024]{2,1,0:T(8,128)(2,1)S(1)}, bf16[4,272,1024]{2,1,0:T(8,128)(2,1)S(1)}, u32[]{:S(2)}, u32[]{:S(2)}) collective-permute-start(bf16[4,272,1024]{2,1,0:T(8,128)(2,1)S(1)} %pad_maximum_fusion), channel_id=1, source_target_pairs={{0,1},{1,0},{2,3},{3,2},{4,5},{5,4},{6,7},{7,6},{8,9},{9,8},{10,11... | collective-permute-start | bytes 6684680 | tf_op jit(solution)/shard_map/ppermute | solution.py:73
  91.8 4.4 %collective-permute-start.8 = (bf16[4,272,1024]{2,1,0:T(8,128)(2,1)S(1)}, bf16[4,272,1024]{2,1,0:T(8,128)(2,1)S(1)}, u32[]{:S(2)}, u32[]{:S(2)}) collective-permute-start(bf16[4,272,1024]{2,1,0:T(8,128)(2,1)S(1)} %pad_maximum_fusion.1), channel_id=1, source_target_pairs={{0,1},{1,0},{2,3},{3,2},{4,5},{5,4},{6,7},{7,6},{8,9},{9,8},{10,11... | collective-permute-start | bytes 6684680 | tf_op jit(solution)/shard_map/ppermute | solution.py:73
  113.5 19.0 %collective-permute-start.11 = (bf16[512,704]{0,1:T(8,128)(2,1)S(1)}, bf16[512,704]{0,1:T(8,128)(2,1)S(1)}, u32[]{:S(2)}, u32[]{:S(2)}) collective-permute-start(bf16[512,704]{0,1:T(8,128)(2,1)S(1)} %convolution_convert_fusion.1), channel_id=1, source_target_pairs={{0,16},{16,0},{1,17},{17,1},{2,18},{18,2},{3,19},{19,3},{4,20},{20... | collective-permute-start | bytes 2162696 | tf_op jit(solution)/shard_map/ppermute | solution.py:118
  115.7 31.5 %collective-permute-start.12 = (bf16[512,704]{0,1:T(8,128)(2,1)S(1)}, bf16[512,704]{0,1:T(8,128)(2,1)S(1)}, u32[]{:S(2)}, u32[]{:S(2)}) collective-permute-start(bf16[512,704]{0,1:T(8,128)(2,1)S(1)} %convolution_convert_fusion), channel_id=1, source_target_pairs={{0,16},{16,0},{1,17},{17,1},{2,18},{18,2},{3,19},{19,3},{4,20},{20... | collective-permute-start | bytes 2162696 | tf_op jit(solution)/shard_map/ppermute | solution.py:118
